TPU v7x, 32 devices: a whole 2x2x4 slice. The times are simulated.
32 devices in a mesh: dp: 8 (over y, x, core), expert: 4 (over z).
Axes of the slice: x: 2, y: 2, z: 4, core: 2. Of those that a mesh axis runs over, the one named last changes fastest.
Arguments:
- layer_input: bfloat16 [4096, 2560], P(('dp', 'expert')), may hold values from -6 to 6
- output_grad: bfloat16 [4096, 2560], P(('dp', 'expert')), may hold values from -6 to 6
- expert_ids: int32 [4096, 2], P(('dp', 'expert')), may hold values from 0 to 3, all different within a row; in each aligned block of 128 rows (0 to 127, 128 to 255, ...) at most 96 rows name the same one
- gate_probs: bfloat16 [4096, 2], P(('dp', 'expert')), may hold values from 0.099609375 to 0.59765625
- gate_weight: float32 [4, 2560, 1536], P('expert', 'dp'), may hold values from -0.125 to 0.125
- up_weight: float32 [4, 2560, 1536], P('expert', 'dp'), may hold values from -0.125 to 0.125
- down_weight: float32 [4, 1536, 2560], P('expert', 'dp'), may hold values from -0.15625 to 0.15625
- gate_moment: float32 [4, 2560, 1536], P('expert', 'dp'), may hold values from -12 to 12
- up_moment: float32 [4, 2560, 1536], P('expert', 'dp'), may hold values from -12 to 12
- down_moment: float32 [4, 1536, 2560], P('expert', 'dp'), may hold values from -12 to 12
- gate_second: float32 [4, 2560, 1536], P('expert', 'dp'), may hold values from 1 to 100
- up_second: float32 [4, 2560, 1536], P('expert', 'dp'), may hold values from 1 to 100
- down_second: float32 [4, 1536, 2560], P('expert', 'dp'), may hold values from 1 to 100
Outputs:
- input_grad: bfloat16 [4096, 2560], P(('dp', 'expert'))
- prob_grad: bfloat16 [4096, 2], P(('dp', 'expert'))
- new_gate_weight: float32 [4, 2560, 1536], P('expert', 'dp')
- new_up_weight: float32 [4, 2560, 1536], P('expert', 'dp')
- new_down_weight: float32 [4, 1536, 2560], P('expert', 'dp')
- new_gate_moment: float32 [4, 2560, 1536], P('expert', 'dp')
- new_up_moment: float32 [4, 2560, 1536], P('expert', 'dp')
- new_down_moment: float32 [4, 1536, 2560], P('expert', 'dp')
- new_gate_second: float32 [4, 2560, 1536], P('expert', 'dp')
- new_up_second: float32 [4, 2560, 1536], P('expert', 'dp')
- new_down_second: float32 [4, 1536, 2560], P('expert', 'dp')
Inputs may be any that keep to these rules, and one draw needn't show every extreme that they name: `expert_ids`: each token names 2 different experts. Among the (token, pick) pairs of one device's 128 tokens, no expert is named more than 96 times, and in every draw some device's tokens name some expert exactly 96 times.
All inputs are finite; a program needn't handle non-finite values.
Results may differ from a plain program's by a relative error of at most 0.025.
Values may be sent and summed in bfloat16 or wider, within the bound.
A program may use at most 256 MiB of HBM per device.

v0:
```python
import jax
import jax.numpy as jnp
from jax import lax
from jax.sharding import PartitionSpec as P

beta_one = 0.9
beta_two = 0.95
learn_rate = 0.003
decay_rate = 0.1
epsilon = 1e-08
correct_one = 1.0 - 2.6561398887587e-05
correct_two = 1.0 - 0.005920529220333


def slot_tables(flat_ids, expert_count, exp_dev, groups, capacity):
    onehot = (flat_ids[:, None] == jnp.arange(expert_count, dtype=jnp.int32)[None, :]).astype(
        jnp.int32
    )
    before = jnp.cumsum(onehot, axis=0) - onehot
    ranked = jnp.sum(before * onehot, axis=1)
    device = flat_ids // exp_dev
    local = flat_ids % exp_dev
    return (local * groups + device) * capacity + ranked


def adamw(weight, moment, second, grad):
    moment_new = beta_one * moment + (1.0 - beta_one) * grad
    second_new = beta_two * second + (1.0 - beta_two) * grad * grad
    update = moment_new / correct_one / (jnp.sqrt(second_new / correct_two) + epsilon)
    return (weight - learn_rate * (update + decay_rate * weight), moment_new, second_new)


def body(
    layer_input,
    output_grad,
    expert_ids,
    gate_probs,
    gate_weight,
    up_weight,
    down_weight,
    gate_moment,
    up_moment,
    down_moment,
    gate_second,
    up_second,
    down_second,
):
    exp_dev = gate_weight.shape[0]
    hidden_units = gate_weight.shape[2]
    width = layer_input.shape[1]
    groups = lax.axis_size("expert")
    shards = lax.axis_size("dp")
    tok_count, picks = expert_ids.shape
    capacity = 3 * tok_count * picks // (2 * exp_dev * groups)
    slots = exp_dev * groups * capacity
    row_count = groups * capacity
    dest_slot = slot_tables(expert_ids.reshape(-1), exp_dev * groups, exp_dev, groups, capacity)
    owner = (
        jnp.zeros((slots,), jnp.int32)
        .at[dest_slot]
        .set(jnp.arange(tok_count * picks, dtype=jnp.int32) // picks)
    )
    filled = jnp.zeros((slots,), jnp.int32).at[dest_slot].set(1) > 0
    zero_val = jnp.zeros((), jnp.bfloat16)
    send_input = jnp.where(filled[:, None], layer_input[owner], zero_val).reshape(
        exp_dev, groups, capacity, width
    )
    send_grad = jnp.where(filled[:, None], output_grad[owner], zero_val).reshape(
        exp_dev, groups, capacity, width
    )
    send_gate = (
        jnp.zeros((slots,), jnp.bfloat16)
        .at[dest_slot]
        .set(gate_probs.reshape(-1))
        .reshape(exp_dev, groups, capacity)
    )
    w_gate_up_shard = jnp.concatenate((gate_weight, up_weight), axis=2).astype(jnp.bfloat16)
    w_down_shard = down_weight.astype(jnp.bfloat16)
    w_gate_up, w_down = (
        lax.all_gather(w_gate_up_shard, "dp", axis=1, tiled=True),
        lax.all_gather(w_down_shard, "dp", axis=1, tiled=True),
    )
    recv_input, recv_grad, recv_gate = (
        lax.all_to_all(send_input, "expert", split_axis=1, concat_axis=1, tiled=True),
        lax.all_to_all(send_grad, "expert", split_axis=1, concat_axis=1, tiled=True),
        lax.all_to_all(send_gate, "expert", split_axis=1, concat_axis=1, tiled=True),
    )
    x_rows = recv_input.reshape(exp_dev, row_count, width)
    dy_rows = recv_grad.reshape(exp_dev, row_count, width)
    gate_rows = recv_gate.reshape(exp_dev, row_count)
    pre = jnp.einsum("erd,edf->erf", x_rows, w_gate_up, preferred_element_type=jnp.float32)
    gate_pre = pre[:, :, :hidden_units]
    up_pre = pre[:, :, hidden_units:]
    sigmoid_gate = jax.nn.sigmoid(gate_pre)
    silu_gate = gate_pre * sigmoid_gate
    hidden = (silu_gate * up_pre).astype(jnp.bfloat16)
    expert_out = jnp.einsum("erf,efd->erd", hidden, w_down, preferred_element_type=jnp.float32)
    prob_rows = jnp.sum(dy_rows.astype(jnp.float32) * expert_out, axis=2).astype(jnp.bfloat16)
    out_scaled = (gate_rows.astype(jnp.float32)[:, :, None] * dy_rows.astype(jnp.float32)).astype(
        jnp.bfloat16
    )
    down_cols = hidden_units // shards
    model_cols = width // shards
    hidden_grad = jnp.einsum("erd,efd->erf", out_scaled, w_down, preferred_element_type=jnp.float32)
    dsilu = sigmoid_gate * (1.0 + gate_pre * (1.0 - sigmoid_gate))
    pre_grad = jnp.concatenate(
        (hidden_grad * up_pre * dsilu, hidden_grad * silu_gate), axis=2
    ).astype(jnp.bfloat16)
    input_rows = jnp.einsum(
        "erf,edf->erd", pre_grad, w_gate_up, preferred_element_type=jnp.float32
    ).astype(jnp.bfloat16)
    cols = x_rows
    first = jnp.einsum("erc,erf->cef", cols, pre_grad, preferred_element_type=jnp.float32).reshape(
        1 * lax.axis_size("dp"), model_cols * exp_dev * 2 * hidden_units
    )
    cols = hidden
    second = jnp.einsum(
        "erc,erd->ced", cols, out_scaled, preferred_element_type=jnp.float32
    ).reshape(1 * lax.axis_size("dp"), down_cols * exp_dev * width)
    joined = lax.psum_scatter(
        jnp.concatenate((first, second), axis=1).astype(jnp.bfloat16),
        "dp",
        scatter_dimension=0,
        tiled=True,
    ).astype(jnp.float32)
    split_at = model_cols * exp_dev * 2 * hidden_units
    grad_gate_up = joined[0, :split_at].reshape(model_cols, exp_dev, 2 * hidden_units)
    grad_down = joined[0, split_at:].reshape(down_cols, exp_dev, width)
    back_input, back_prob = (
        lax.all_to_all(
            input_rows.reshape(exp_dev, groups, capacity, width),
            "expert",
            split_axis=1,
            concat_axis=1,
            tiled=True,
        ),
        lax.all_to_all(
            prob_rows.reshape(exp_dev, groups, capacity),
            "expert",
            split_axis=1,
            concat_axis=1,
            tiled=True,
        ),
    )
    picked_rows = back_input.reshape(slots, width)[dest_slot].reshape(tok_count, picks, width)
    input_grad = jnp.sum(picked_rows.astype(jnp.float32), axis=1).astype(jnp.bfloat16)
    prob_grad = back_prob.reshape(slots)[dest_slot].reshape(tok_count, picks)
    grad_gate_up = jnp.transpose(grad_gate_up, (1, 0, 2))
    grad_down = jnp.transpose(grad_down, (1, 0, 2))
    new_gate_weight, new_gate_moment, new_gate_second = adamw(
        gate_weight, gate_moment, gate_second, grad_gate_up[:, :, :hidden_units]
    )
    new_up_weight, new_up_moment, new_up_second = adamw(
        up_weight, up_moment, up_second, grad_gate_up[:, :, hidden_units:]
    )
    new_down_weight, new_down_moment, new_down_second = adamw(
        down_weight, down_moment, down_second, grad_down
    )
    return (
        input_grad,
        prob_grad,
        new_gate_weight,
        new_up_weight,
        new_down_weight,
        new_gate_moment,
        new_up_moment,
        new_down_moment,
        new_gate_second,
        new_up_second,
        new_down_second,
    )


def solution(mesh):
    return jax.shard_map(
        body,
        mesh=mesh,
        in_specs=(
            P(("dp", "expert"), None),
            P(("dp", "expert"), None),
            P(("dp", "expert"), None),
            P(("dp", "expert"), None),
            P("expert", "dp", None),
            P("expert", "dp", None),
            P("expert", "dp", None),
            P("expert", "dp", None),
            P("expert", "dp", None),
            P("expert", "dp", None),
            P("expert", "dp", None),
            P("expert", "dp", None),
            P("expert", "dp", None),
        ),
        out_specs=(
            P(("dp", "expert"), None),
            P(("dp", "expert"), None),
            P("expert", "dp", None),
            P("expert", "dp", None),
            P("expert", "dp", None),
            P("expert", "dp", None),
            P("expert", "dp", None),
            P("expert", "dp", None),
            P("expert", "dp", None),
            P("expert", "dp", None),
            P("expert", "dp", None),
        ),
        check_vma=False,
    )
```

profile of v0, /device:TPU:0, one launch (start us, length us, event | category | flops | bytes accessed | tf_op | source)
XLA Modules:
  0.0 663.4 jit_solution(8616133354549661937)
XLA Ops:
  19.1 6.3 all-to-all-start
  38.1 49.9 %all_to_all.25 = bf16[1,4,96,2560]{3,2,0,1:T(8,128)(2,1)S(1)} all-to-all(bf16[1,4,96,2560]{3,2,0,1:T(8,128)(2,1)} %get-tuple-element.60), channel_id=1, replica_groups=mesh['dp'=8,'expert'=4] {'expert'}, dimensions={1} | all-to-all | bytes 3932160 | tf_op jit(solution)/shard_map/all_to_all | solution.py:85
  95.3 41.7 %all-to-all-done.2 = bf16[1,4,96,2560]{3,2,0,1:T(8,128)(2,1)} async-done(((bf16[1,4,96,2560]{3,2,0,1:T(8,128)(2,1)}), bf16[1,4,96,2560]{3,2,0,1:T(8,128)(2,1)}, u32[]{:S(2)}, u32[]{:S(2)}) %all-to-all-start.2) | async-done | bytes 1966112 | tf_op jit(solution)/shard_map/all_to_all | solution.py:84
  136.9 11.9 %fusion.13 = f32[1,384,3072]{2,1,0:T(8,128)} fusion(bf16[384,2560]{1,0:T(8,128)(2,1)} %bitcast.12, bf16[1,2560,3072]{2,1,0:T(8,128)(2,1)} %all-gather.5.cloned.1.call-done), kind=kOutput, calls=%fused_computation.22 | convolution fusion | flops 6039797760 | bytes 22413312 | tf_op jit(solution)/shard_map/erd,edf->erf/dot_general | solution.py:91
  148.8 5.2 all-gather.3.cloned.1.call-done
  154.0 10.7 %fusion.32 = (bf16[384,1536]{1,0:T(8,128)(2,1)S(1)}, bf16[384,1536]{1,0:T(8,128)(2,1)}, bf16[384,1536]{1,0:T(8,128)(2,1)S(1)}) fusion(f32[1,384,3072]{2,1,0:T(8,128)} %fusion.13, bf16[1,1536,2560]{2,1,0:T(8,128)(2,1)} %all-gather.3.cloned.1.call-done, f32[1,384,1,1,1,1,2560]{6,1,5,4,3,2,0:T(8,128)} %bitcast.94, f32[384]{0:T(512)S(1)} %reshape.356), kind=kOutput, calls=%fused_computation.53 | convolution fusion | flops 3030712320 | bytes 20055552 | tf_op jit(solution)/shard_map/erd,efd->erf/dot_general | solution.py:104
  164.7 6.6 fusion.5
  171.4 10.6 %copy.59 = bf16[1536,1,2560]{2,0,1:T(8,128)(2,1)} copy(bf16[1536,1,2560]{0,2,1:T(8,128)(2,1)} %fusion.5) | data formatting | bytes 15728640 | tf_op jit(solution)/shard_map/erc,erd->ced/transpose | solution.py:117
  182.0 9.9 %reshape.355 = bf16[8,491520]{1,0:T(8,128)(2,1)} reshape(bf16[1536,1,2560]{2,0,1:T(8,128)(2,1)} %copy.59) | data formatting | bytes 15728640 | tf_op jit(solution)/shard_map/reshape | solution.py:119
  191.9 13.8 %fusion.4 = bf16[2560,1,3072]{0,2,1:T(8,128)(2,1)} fusion(bf16[384,2560]{1,0:T(8,128)(2,1)} %bitcast.12, bf16[384,1536]{1,0:T(8,128)(2,1)} %get-tuple-element.54, bf16[384,1536]{1,0:T(8,128)(2,1)S(1)} %get-tuple-element.53), kind=kOutput, calls=%fused_computation.13 | convolution fusion | flops 6052380672 | bytes 20054016 | tf_op jit(solution)/shard_map/erc,erf->cef/dot_general | solution.py:113
  205.6 20.7 %copy.58 = bf16[2560,1,3072]{2,0,1:T(8,128)(2,1)} copy(bf16[2560,1,3072]{0,2,1:T(8,128)(2,1)} %fusion.4) | data formatting | bytes 31457280 | tf_op jit(solution)/shard_map/erc,erf->cef/transpose | solution.py:113
  226.3 18.1 %reshape.354 = bf16[8,983040]{1,0:T(8,128)(2,1)} reshape(bf16[2560,1,3072]{2,0,1:T(8,128)(2,1)} %copy.58) | data formatting | bytes 31457280 | tf_op jit(solution)/shard_map/reshape | solution.py:113
  244.4 23.8 %pad_maximum_fusion = bf16[8,1474560]{1,0:T(8,128)(2,1)} fusion(bf16[8,491520]{1,0:T(8,128)(2,1)} %reshape.355, bf16[8,983040]{1,0:T(8,128)(2,1)} %reshape.354), kind=kLoop, calls=%fused_computation.7 | loop fusion | flops 47185920 | bytes 47185920 | tf_op jit(solution)/shard_map/concatenate | solution.py:121
  268.2 7.6 %fusion.27 = bf16[384]{0:T(512)(128)(2,1)S(1)} fusion(f32[384,2560]{1,0:T(8,128)} %bitcast.95, bf16[384,1536]{1,0:T(8,128)(2,1)S(1)} %get-tuple-element.55, bf16[1,1536,2560]{2,1,0:T(8,128)(2,1)} %all-gather.3.cloned.1.call-done), kind=kOutput, calls=%fused_computation.50 | convolution fusion | flops 3021864448 | bytes 12976896 | tf_op jit(solution)/shard_map/erf,efd->erd/dot_general | solution.py:97
  281.1 11.1 %fusion.16 = bf16[384,2560]{1,0:T(8,128)(2,1)} fusion(bf16[1,2560,3072]{2,1,0:T(8,128)(2,1)} %all-gather.5.cloned.1.call-done, bf16[384,1536]{1,0:T(8,128)(2,1)} %get-tuple-element.54, bf16[384,1536]{1,0:T(8,128)(2,1)S(1)} %get-tuple-element.53), kind=kOutput, calls=%fused_computation.23 | convolution fusion | flops 6045499392 | bytes 20054016 | tf_op jit(solution)/shard_map/erf,edf->erd/dot_general | solution.py:109
  292.2 5.2 all-to-all-start.3
  300.8 41.9 %all-to-all-done.3 = bf16[1,4,96,2560]{3,2,0,1:T(8,128)(2,1)S(1)} async-done(((bf16[1,4,96,2560]{3,2,0,1:T(8,128)(2,1)}), bf16[1,4,96,2560]{3,2,0,1:T(8,128)(2,1)S(1)}, u32[]{:S(2)}, u32[]{:S(2)}) %all-to-all-start.3) | async-done | bytes 1966112 | tf_op jit(solution)/shard_map/all_to_all | solution.py:130
  352.7 206.2 %all-reduce.3.cloned.1.call-done = bf16[8,1474560]{1,0:T(8,128)(2,1)} async-done(((bf16[8,1474560]{1,0:T(8,128)(2,1)}), bf16[8,1474560]{1,0:T(8,128)(2,1)}) %all-reduce.3.cloned.1.call-update) | async-done | bytes 23592976
  558.8 10.3 %dynamic-slice_convert_fusion = f32[1,1474560]{1,0:T(1,128)S(1)} fusion(bf16[8,1474560]{1,0:T(8,128)(2,1)} %all-reduce.3.cloned.1.call-done, u32[]{:T(128)} %bitcast.31), kind=kLoop, calls=%fused_computation.20 | loop fusion | flops 1474560 | bytes 8847364 | tf_op jit(solution)/shard_map/convert_element_type | solution.py:125
  569.2 42.4 %slice_reduce_fusion = f32[983040]{0:T(1024)} fusion(f32[1,1474560]{1,0:T(1,128)S(1)} %dynamic-slice_convert_fusion), kind=kLoop, calls=%fused_computation.24 | loop fusion | bytes 7864320 | tf_op jit(solution)/shard_map/slice | solution.py:127
  611.6 21.8 %slice_reduce_fusion.1 = f32[491520]{0:T(1024)} fusion(f32[1,1474560]{1,0:T(1,128)S(1)} %dynamic-slice_convert_fusion), kind=kLoop, calls=%fused_computation.40 | loop fusion | bytes 3932160 | tf_op jit(solution)/shard_map/slice | solution.py:128
  633.4 4.9 transpose_reshape_squeeze.6
  641.1 6.6 multiply_subtract_fusion
  650.0 6.7 %multiply_subtract_fusion.1 = (f32[1,320,1536]{2,1,0:T(8,128)}, f32[1,320,1536]{2,1,0:T(8,128)}, f32[1,320,1536]{2,1,0:T(8,128)}, f32[1,320,1536]{2,1,0:T(8,128)...) fusion(f32[1,320,1536]{2,1,0:T(8,128)S(1)} %copy-done.6, f32[1,320,3072]{2,1,0:T(8,128)S(1)} %copy-done.3, ...), kind=kLoop, calls=%fused_computation.44 | loop fusion | flops 14745600 | bytes 27525120 | tf_op jit(solution)/shard_map/sub | solution.py:30
  (93 shorter events, 55.3 us)
Async XLA Ops:
  7.2 21.2 %copy-start = (bf16[128,2560]{1,0:T(8,128)(2,1)S(1)}, bf16[128,2560]{1,0:T(8,128)(2,1)}, u32[]{:S(2)}) copy-start(bf16[128,2560]{1,0:T(8,128)(2,1)} %param.13) | copy-start | bytes 1966084
  7.2 2.2 copy-start.7
  7.2 129.7 %all-gather.5.cloned.1.call-start = ((), (), s32[]{:S(2)}) async-start(), calls=%async_computation.6 | async-start | bytes 17694720 | tf_op jit(solution)/shard_map/all_gather | solution.py:80
  11.0 1.5 copy-start.4
  11.0 2.6 copy-start.13
  11.0 4.8 copy-start.14
  11.1 142.9 %all-gather.3.cloned.1.call-start = ((), (), s32[]{:S(2)}) async-start(), calls=%async_computation.5 | async-start | bytes 8847360 | tf_op jit(solution)/shard_map/all_gather | solution.py:81
  19.1 19.0 %all-to-all-start = ((bf16[1,4,96]{2,0,1:T(2,128)(2,1)}), bf16[1,4,96]{2,0,1:T(2,128)(2,1)S(1)}, u32[]{:S(2)}, u32[]{:S(2)}) async-start(bf16[1,4,96]{2,0,1:T(2,128)(2,1)} %reshape.417), calls=%async_computation | async-start | bytes 4096 | tf_op jit(solution)/shard_map/all_to_all | solution.py:86
  28.3 2.6 copy-start.2
  88.0 48.9 %all-to-all-start.2 = ((bf16[1,4,96,2560]{3,2,0,1:T(8,128)(2,1)}), bf16[1,4,96,2560]{3,2,0,1:T(8,128)(2,1)}, u32[]{:S(2)}, u32[]{:S(2)}) async-start(bf16[1,4,96,2560]{3,2,0,1:T(8,128)(2,1)} %get-tuple-element.59), calls=%async_computation.2 | async-start | bytes 3932160 | tf_op jit(solution)/shard_map/all_to_all | solution.py:84
  92.4 466.4 %all-reduce.3.cloned.1.call-start = ((), (), s32[]{:S(2)}) async-start(), calls=%async_computation.7 | async-start | bytes 47185920
  154.0 10.8 %copy-start.9 = (f32[1,4,96,2560]{3,2,0,1:T(8,128)S(1)}, f32[1,4,96,2560]{3,2,0,1:T(8,128)}, u32[]{:S(2)}) copy-start(f32[1,4,96,2560]{3,2,0,1:T(8,128)} %convert_element_type.140) | copy-start | bytes 11796484
  276.5 15.7 %all-to-all-start.4 = ((bf16[1,4,96]{2,0,1:T(2,128)(2,1)}), bf16[1,4,96]{2,0,1:T(2,128)(2,1)S(1)}, u32[]{:S(2)}, u32[]{:S(2)}) async-start(bf16[1,4,96]{2,0,1:T(2,128)(2,1)} %convert_element_type.142), calls=%async_computation.4 | async-start | bytes 4096 | tf_op jit(solution)/shard_map/all_to_all | solution.py:137
  292.2 5.2 copy-start.15
  292.2 50.5 %all-to-all-start.3 = ((bf16[1,4,96,2560]{3,2,0,1:T(8,128)(2,1)}), bf16[1,4,96,2560]{3,2,0,1:T(8,128)(2,1)S(1)}, u32[]{:S(2)}, u32[]{:S(2)}) async-start(bf16[1,4,96,2560]{3,2,0,1:T(8,128)(2,1)} %bitcast.97), calls=%async_computation.3 | async-start | bytes 3932160 | tf_op jit(solution)/shard_map/all_to_all | solution.py:130
  638.3 2.8 copy-start.5
  641.1 6.6 copy-start.3
  641.1 6.6 %copy-start.6 = (f32[1,320,1536]{2,1,0:T(8,128)S(1)}, f32[1,320,1536]{2,1,0:T(8,128)}, u32[]{:S(2)}) copy-start(f32[1,320,1536]{2,1,0:T(8,128)} %param.18) | copy-start | bytes 5898244
  641.1 6.6 copy-start.8
  641.1 7.7 %copy-start.10 = (f32[1,320,1536]{2,1,0:T(8,128)S(1)}, f32[1,320,1536]{2,1,0:T(8,128)}, u32[]{:S(2)}) copy-start(f32[1,320,1536]{2,1,0:T(8,128)} %param.21) | copy-start | bytes 5898244
  641.1 8.3 %copy-start.11 = (f32[1,320,1536]{2,1,0:T(8,128)S(1)}, f32[1,320,1536]{2,1,0:T(8,128)}, u32[]{:S(2)}) copy-start(f32[1,320,1536]{2,1,0:T(8,128)} %param.24) | copy-start | bytes 5898244
  641.1 8.8 %copy-start.12 = (f32[1,320,1536]{2,1,0:T(8,128)S(1)}, f32[1,320,1536]{2,1,0:T(8,128)}, u32[]{:S(2)}) copy-start(f32[1,320,1536]{2,1,0:T(8,128)} %param.23) | copy-start | bytes 5898244
  650.0 6.7 %copy-start.1 = (bf16[128,2560]{1,0:T(8,128)(2,1)S(1)}, bf16[128,2560]{1,0:T(8,128)(2,1)}, u32[]{:S(2)}) copy-start(bf16[128,2560]{1,0:T(8,128)(2,1)} %param.13) | copy-start | bytes 1966084
Sparse Core Ops, SparseCore 0:
  11.2 88.1 all-gather.4
  101.8 52.1 all-gather.2
  268.3 290.5 all-reduce.2
where the time goes:
time: 671 us; the launch traced here: 663 us
  waiting for transfers between devices  295 us (44%)
  local copies, waits for them, and re-layouts  158 us (24%)
  other arithmetic  63.9 us (10%)
  matrix products  61.8 us (9%)
  blocking collectives  49.9 us (7%)
  starting transfers between devices  20.9 us (3%)
  between operations  14.2 us (2%)
    unnamed x4, waiting for transfers between devices  206 us
    all_to_all x1, blocking collectives, body(): lax.all_to_all(send_grad, 'expert', split_axis=1, concat_axis=1, tiled=True)  49.9 us
    slice x1, local copies, waits for them, and re-layouts, body(): joined[0, :split_at].reshape(model_cols, exp_dev, 2 * hidden_units)  42.4 us
    all_to_all x1, waiting for transfers between devices, body(): lax.all_to_all(input_rows.reshape(exp_dev, groups, capacity, width), 'exp...  41.9 us
    all_to_all x1, waiting for transfers between devices, body(): lax.all_to_all(send_input, 'expert', split_axis=1, concat_axis=1, tiled=T...  41.7 us
    concatenate x1, other arithmetic, body(): jnp.concatenate((first, second), axis=1).astype(jnp.bfloat16)  23.8 us
    slice x1, local copies, waits for them, and re-layouts, body(): grad_down = joined[0, split_at:].reshape(down_cols, exp_dev, width)  21.8 us
    transpose x1, local copies, waits for them, and re-layouts, body(): jnp.einsum('erc,erf->cef', cols, pre_grad, preferred_element_type=jnp.flo...  20.7 us
  transfers between devices with their start and end apart: 7, of which 4 were waited for; matrix products, arithmetic and copies ran while one was open for 10% of the time, Pallas kernels for 0%

commit v1 on v0

--- a/solution.py
+++ b/solution.py
@@ -1,6 +1,10 @@
+import functools
+
 import jax
 import jax.numpy as jnp
 from jax import lax
+from jax.experimental import pallas as pl
+from jax.experimental.pallas import tpu as pltpu
 from jax.sharding import PartitionSpec as P
 
 beta_one = 0.9
@@ -171,9 +175,446 @@
     )
 
 
+MESH = pl.DeviceIdType.MESH
+A_PIECES, B_PIECES = (0, 1, 2), (3, 4, 5)
+
+
+def place():
+    me = lax.axis_index("dp")
+    z = lax.axis_index("expert")
+    core, col, row = me % 2, (me // 2) % 2, me // 4
+    sib = me + 1 - 2 * core
+    return me, z, sib, 2 - 4 * col, 4 - 8 * row
+
+
+def enter(me, z, depth, peers, others):
+    barrier = pltpu.get_barrier_semaphore()
+    for peer in peers:
+        pl.semaphore_signal(barrier, inc=1, device_id=(peer, z), device_id_type=MESH)
+    for other in others:
+        pl.semaphore_signal(barrier, inc=1, device_id=(me, other), device_id_type=MESH)
+    pl.semaphore_wait(barrier, len(peers) + len(others))
+
+
+def remote(src, dst, send, recv, device):
+    return pltpu.make_async_remote_copy(
+        src_ref=src, dst_ref=dst, send_sem=send, recv_sem=recv, device_id=device, device_id_type=MESH
+    )
+
+
+def piece_at(k, joined, down, block, rows, down_rows, hidden):
+    half, part = k // 3, k % 3
+    if part == 2:
+        n = down_rows // 2
+        return down.at[pl.ds(pl.multiple_of(block * down_rows + half * n, 16), n)]
+    n = rows // 2
+    return joined.at[
+        pl.ds(pl.multiple_of(block * rows + part * n, 16), n), pl.ds(half * hidden, hidden)
+    ]
+
+
+def gather_kernel(
+    depth, x, y, gm, wgu, wd, out_wgu, out_wd, out_x, out_y, out_gm, ssem, rsem, zsend, zrecv, lsem
+):
+    me, z, sib, dx, dy = place()
+    rows, hidden, down_rows, toks = wgu.shape[0], wgu.shape[1] // 2, wd.shape[0], x.shape[0]
+    enter(me, z, depth, (sib, me + dx, me + dy), ((z + 1) % depth, (z + depth - 1) % depth))
+
+    def own(k):
+        return piece_at(k, wgu, wd, 0, rows, down_rows, hidden)
+
+    def at(k, block):
+        return piece_at(k, out_wgu, out_wd, block, rows, down_rows, hidden)
+
+    sends = []
+
+    def send(src, k, block, kind, rel, peer):
+        copy = remote(src, at(k, block), ssem.at[kind, k], rsem.at[rel, k], (peer, z))
+        copy.start()
+        sends.append(copy)
+
+    def arrived(k, block, rel):
+        remote(at(k, block), at(k, block), ssem.at[0, k], rsem.at[rel, k], (sib, z)).wait_recv()
+
+    ins, outs = (x, y, gm), (out_x, out_y, out_gm)
+
+    def zat(k, block):
+        return outs[k].at[pl.ds(pl.multiple_of(block * toks, 16), toks)]
+
+    def zcopy(way, d, k):
+        sign = 1 - 2 * way
+        block = z - sign * (d - 1)
+        src = ins[k] if d == 1 else zat(k, block)
+        return remote(src, zat(k, block), zsend.at[way, d - 1, k], zrecv.at[way, d - 1, k], (me, z + sign))
+
+    def zwait(way, d, k):
+        block = z - (1 - 2 * way) * d
+        remote(
+            zat(k, block), zat(k, block), zsend.at[way, d - 1, k], zrecv.at[way, d - 1, k], (me, (z + 1) % depth)
+        ).wait_recv()
+
+    def hop(d, k):
+        @pl.when(z >= d)
+        def _():
+            zwait(0, d, k)
+            if d < depth - 1:
+
+                @pl.when(z < depth - 1)
+                def _():
+                    zcopy(0, d + 1, k).start()
+
+        @pl.when(z + d <= depth - 1)
+        def _():
+            zwait(1, d, k)
+            if d < depth - 1:
+
+                @pl.when(z > 0)
+                def _():
+                    zcopy(1, d + 1, k).start()
+
+    for i in range(3):
+        send(own(A_PIECES[i]), A_PIECES[i], me, 0, 2, me + dx)
+        send(own(B_PIECES[i]), B_PIECES[i], me, 1, 4, me + dy)
+
+    @pl.when(z < depth - 1)
+    def _():
+        for k in (2, 0, 1):
+            zcopy(0, 1, k).start()
+
+    @pl.when(z > 0)
+    def _():
+        for k in (2, 0, 1):
+            zcopy(1, 1, k).start()
+
+    for i in range(3):
+        send(own(B_PIECES[i]), B_PIECES[i], me, 0, 2, me + dx)
+        send(own(A_PIECES[i]), A_PIECES[i], me, 1, 4, me + dy)
+    for k in range(6):
+        send(own(k), k, me, 2, 1, sib)
+    local = [pltpu.make_async_copy(own(k), at(k, me), lsem.at[k]) for k in range(6)]
+    local += [pltpu.make_async_copy(ins[k], zat(k, z), lsem.at[6 + k]) for k in range(3)]
+    for copy in local:
+        copy.start()
+
+    for i in range(3):
+        ka, kb = A_PIECES[i], B_PIECES[i]
+        arrived(ka, me + dx, 2)
+        send(at(ka, me + dx), ka, me + dx, 3, 6, me + dy)
+        send(at(ka, me + dx), ka, me + dx, 4, 3, sib)
+        arrived(kb, me + dy, 4)
+        send(at(kb, me + dy), kb, me + dy, 3, 6, me + dx)
+        send(at(kb, me + dy), kb, me + dy, 5, 5, sib)
+        if i == 0:
+            hop(1, 2)
+        if i == 1:
+            hop(1, 0)
+    hop(1, 1)
+    hop(2, 2)
+    for i in range(3):
+        ka, kb = A_PIECES[i], B_PIECES[i]
+        arrived(kb, me + dx, 2)
+        send(at(kb, me + dx), kb, me + dx, 4, 3, sib)
+        arrived(ka, me + dy, 4)
+        send(at(ka, me + dy), ka, me + dy, 5, 5, sib)
+        if i == 1:
+            hop(2, 0)
+    hop(2, 1)
+    for k in (0, 3, 1, 4, 2, 5):
+        arrived(k, me + dx + dy, 6)
+        send(at(k, me + dx + dy), k, me + dx + dy, 6, 7, sib)
+    for k in (2, 0, 1):
+        hop(3, k)
+    for k in range(6):
+        arrived(k, sib, 1)
+        arrived(k, sib + dx, 3)
+        arrived(k, sib + dy, 5)
+        arrived(k, sib + dx + dy, 7)
+    for copy in sends:
+        copy.wait_send()
+    for copy in local:
+        copy.wait()
+    for d in range(1, depth):
+        for k in range(3):
+
+            @pl.when((z < depth - 1) & (z >= d - 1))
+            def _():
+                zcopy(0, d, k).wait_send()
+
+            @pl.when((z > 0) & (z + d - 1 <= depth - 1))
+            def _():
+                zcopy(1, d, k).wait_send()
+
+
+def scatter_kernel(
+    depth,
+    p13,
+    p2,
+    xr,
+    q,
+    g13,
+    g2,
+    out_x,
+    out_q,
+    own_w,
+    own_d,
+    sib_w,
+    sib_d,
+    hop_w,
+    hop_d,
+    s_send,
+    s_recv,
+    load,
+    h_send,
+    h_recv,
+    z_send,
+    z_recv,
+    z_local,
+):
+    me, z, sib, dx, dy = place()
+    rows, hidden, down_rows, toks = g13.shape[0], g13.shape[1] // 2, g2.shape[0], out_x.shape[1]
+    enter(me, z, depth, (sib, me + dx, me + dy), [(z + d) % depth for d in range(1, depth)])
+    shift = (0, dx, dy, dx + dy)
+
+    def part(k, block):
+        return piece_at(k, p13, p2, block, rows, down_rows, hidden)
+
+    def slot(wide, narrow, j, k):
+        half, i = k // 3, k % 3
+        return narrow.at[j, half] if i == 2 else wide.at[j, 2 * half + i]
+
+    def hopped(kind, k):
+        i = k % 3
+        return hop_d.at[kind] if i == 2 else hop_w.at[kind, i]
+
+    order = [(3, k) for k in (0, 3, 1, 4, 2, 5)]
+    order += [(1, 0), (2, 3), (1, 1), (2, 4), (1, 2), (2, 5)]
+    order += [(2, 0), (1, 3), (2, 1), (1, 4), (2, 2), (1, 5)]
+    order += [(0, k) for k in (0, 3, 1, 4, 2, 5)]
+    pair, loads = {}, {}
+    for j, k in order:
+        pair[j, k] = remote(
+            part(k, sib + shift[j]),
+            slot(sib_w, sib_d, j, k),
+            s_send.at[j, k],
+            s_recv.at[j, k],
+            (sib, z),
+        )
+        pair[j, k].start()
+        loads[j, k] = pltpu.make_async_copy(
+            part(k, me + shift[j]), slot(own_w, own_d, j, k), load.at[j, k]
+        )
+        loads[j, k].start()
+
+    zcopies = []
+    for d in range(1, depth):
+        to = (z + d) % depth
+        block = pl.ds(pl.multiple_of(to * toks, 16), toks)
+        for n, (src, dst) in enumerate(((xr, out_x), (q, out_q))):
+            copy = remote(
+                src.at[block], dst.at[z], z_send.at[d - 1, n], z_recv.at[d - 1, n], (me, to)
+            )
+            copy.start()
+            zcopies.append(copy)
+    mine = pl.ds(pl.multiple_of(z * toks, 16), toks)
+    zlocal = [
+        pltpu.make_async_copy(src.at[mine], dst.at[z], z_local.at[n])
+        for n, (src, dst) in enumerate(((xr, out_x), (q, out_q)))
+    ]
+    for copy in zlocal:
+        copy.start()
+
+    def add(dst, terms):
+        def step(i, _):
+            at = pl.ds(pl.multiple_of(i * 16, 16), 16)
+            total = terms[0][at, :].astype(jnp.float32)
+            for term in terms[1:]:
+                total = total + term[at, :].astype(jnp.float32)
+            dst[at, :] = total.astype(dst.dtype)
+            return 0
+
+        lax.fori_loop(0, dst.shape[0] // 16, step, 0)
+
+    hops = {}
+
+    def hop(kind, k, j, peer):
+        copy = remote(
+            slot(own_w, own_d, j, k),
+            hopped(kind, k),
+            h_send.at[kind, k % 3],
+            h_recv.at[kind, k % 3],
+            (peer, z),
+        )
+        copy.start()
+        hops[kind, k % 3] = copy
+
+    def terms_of(j, k):
+        loads[j, k].wait()
+        pair[j, k].wait_recv()
+        return [slot(own_w, own_d, j, k), slot(sib_w, sib_d, j, k)]
+
+    for i in range(3):
+        for k, kind, peer in ((A_PIECES[i], 0, me + dx), (B_PIECES[i], 3, me + dy)):
+            add(slot(own_w, own_d, 3, k), terms_of(3, k))
+            hop(kind, k, 3, peer)
+    for i in range(3):
+        for k, j, kind, peer in ((A_PIECES[i], 1, 1, me + dx), (B_PIECES[i], 2, 4, me + dy)):
+            add(slot(own_w, own_d, j, k), terms_of(j, k))
+            hop(kind, k, j, peer)
+    for i in range(3):
+        for k, j, came, kind, peer in (
+            (A_PIECES[i], 2, 0, 5, me + dy),
+            (B_PIECES[i], 1, 3, 2, me + dx),
+        ):
+            terms = terms_of(j, k)
+            hops[came, i].wait_recv()
+            add(slot(own_w, own_d, j, k), terms + [hopped(came, k)])
+            hop(kind, k, j, peer)
+    for i in range(3):
+        for k, first, last in ((A_PIECES[i], 1, 5), (B_PIECES[i], 4, 2)):
+            half, n = k // 3, down_rows // 2
+            if i == 2:
+                dst = g2.at[pl.ds(half * n, n)]
+            else:
+                n = rows // 2
+                dst = g13.at[pl.ds(i * n, n), pl.ds(half * hidden, hidden)]
+            terms = terms_of(0, k)
+            hops[first, i].wait_recv()
+            hops[last, i].wait_recv()
+            add(dst, terms + [hopped(first, k), hopped(last, k)])
+    for copy in zcopies:
+        copy.wait()
+    for copy in zlocal:
+        copy.wait()
+    for copy in pair.values():
+        copy.wait_send()
+    for copy in hops.values():
+        copy.wait_send()
+
+
+def block_body(
+    layer_input,
+    output_grad,
+    expert_ids,
+    gate_probs,
+    gate_weight,
+    up_weight,
+    down_weight,
+    gate_moment,
+    up_moment,
+    down_moment,
+    gate_second,
+    up_second,
+    down_second,
+):
+    depth, shards = lax.axis_size("expert"), lax.axis_size("dp")
+    toks, width = layer_input.shape
+    rows, hidden_units = gate_weight.shape[1:]
+    down_rows = down_weight.shape[1]
+    bf16, f32 = jnp.bfloat16, jnp.float32
+    any_spec = pl.BlockSpec(memory_space=pl.ANY)
+    vmem_spec = pl.BlockSpec(memory_space=pltpu.VMEM)
+    dma = pltpu.SemaphoreType.DMA
+
+    lanes = jnp.arange(128, dtype=jnp.int32)
+    named = expert_ids[:, :, None] == lanes[None, None, :]
+    zero = jnp.zeros((), bf16)
+    gate_table = jnp.sum(jnp.where(named, gate_probs[:, :, None], zero), axis=1)
+    w_shard = jnp.concatenate((gate_weight[0], up_weight[0]), axis=1).astype(bf16)
+    w_gate_up, w_down, x_rows, dy_rows, gate_rows = pl.pallas_call(
+        functools.partial(gather_kernel, depth),
+        out_shape=(
+            jax.ShapeDtypeStruct((shards * rows, 2 * hidden_units), bf16),
+            jax.ShapeDtypeStruct((shards * down_rows, width), bf16),
+            jax.ShapeDtypeStruct((depth * toks, width), bf16),
+            jax.ShapeDtypeStruct((depth * toks, width), bf16),
+            jax.ShapeDtypeStruct((depth * toks, 128), bf16),
+        ),
+        in_specs=[any_spec] * 5,
+        out_specs=(any_spec,) * 5,
+        scratch_shapes=[
+            dma((7, 6)),
+            dma((8, 6)),
+            dma((2, depth - 1, 3)),
+            dma((2, depth - 1, 3)),
+            dma((9,)),
+        ],
+        compiler_params=pltpu.CompilerParams(collective_id=0, has_side_effects=True),
+    )(layer_input, output_grad, gate_table, w_shard, down_weight[0].astype(bf16))
+
+    expert = lax.axis_index("expert")
+    gate = jnp.sum(
+        jnp.where(lanes[None, :] == expert, gate_rows.astype(f32), 0.0), axis=1, keepdims=True
+    )
+    out_scaled = (gate * dy_rows.astype(f32)).astype(bf16)
+    pre = jnp.dot(x_rows, w_gate_up, preferred_element_type=f32)
+    gate_pre, up_pre = pre[:, :hidden_units], pre[:, hidden_units:]
+    sigmoid_gate = jax.nn.sigmoid(gate_pre)
+    silu_gate = gate_pre * sigmoid_gate
+    hidden = (silu_gate * up_pre).astype(bf16)
+    expert_out = jnp.dot(hidden, w_down, preferred_element_type=f32)
+    prob_rows = jnp.sum(dy_rows.astype(f32) * expert_out, axis=1, keepdims=True).astype(bf16)
+    nt = (((1,), (1,)), ((), ()))
+    tn = (((0,), (0,)), ((), ()))
+    hidden_grad = lax.dot_general(out_scaled, w_down, nt, preferred_element_type=f32)
+    dsilu = sigmoid_gate * (1.0 + gate_pre * (1.0 - sigmoid_gate))
+    pre_grad = jnp.concatenate(
+        (hidden_grad * up_pre * dsilu, hidden_grad * silu_gate), axis=1
+    ).astype(bf16)
+    input_rows = lax.dot_general(pre_grad, w_gate_up, nt, preferred_element_type=f32).astype(bf16)
+    part_gate_up = lax.dot_general(x_rows, pre_grad, tn, preferred_element_type=f32).astype(bf16)
+    part_down = lax.dot_general(hidden, out_scaled, tn, preferred_element_type=f32).astype(bf16)
+
+    half, half_down = rows // 2, down_rows // 2
+    vm = pltpu.VMEM
+    grad_gate_up, grad_down, back_input, back_prob = pl.pallas_call(
+        functools.partial(scatter_kernel, depth),
+        out_shape=(
+            jax.ShapeDtypeStruct((rows, 2 * hidden_units), f32),
+            jax.ShapeDtypeStruct((down_rows, width), f32),
+            jax.ShapeDtypeStruct((depth, toks, width), bf16),
+            jax.ShapeDtypeStruct((depth, toks, 128), bf16),
+        ),
+        in_specs=[any_spec] * 4,
+        out_specs=(vmem_spec, vmem_spec, any_spec, any_spec),
+        scratch_shapes=[
+            vm((4, 4, half, hidden_units), bf16),
+            vm((4, 2, half_down, width), bf16),
+            vm((4, 4, half, hidden_units), bf16),
+            vm((4, 2, half_down, width), bf16),
+            vm((6, 2, half, hidden_units), bf16),
+            vm((6, half_down, width), bf16),
+            dma((4, 6)),
+            dma((4, 6)),
+            dma((4, 6)),
+            dma((6, 3)),
+            dma((6, 3)),
+            dma((depth - 1, 2)),
+            dma((depth - 1, 2)),
+            dma((2,)),
+        ],
+        compiler_params=pltpu.CompilerParams(
+            collective_id=1, has_side_effects=True, vmem_limit_bytes=56 * 1024 * 1024
+        ),
+    )(part_gate_up, part_down, input_rows, jnp.broadcast_to(prob_rows, (depth * toks, 128)))
+
+    input_grad = jnp.sum(back_input.astype(f32), axis=0).astype(bf16)
+    probs = back_prob[:, :, 0].T
+    prob_grad = jnp.sum(
+        jnp.where(named[:, :, :depth], probs[:, None, :].astype(f32), 0.0), axis=2
+    ).astype(bf16)
+    new_gate = adamw(gate_weight, gate_moment, gate_second, grad_gate_up[None, :, :hidden_units])
+    new_up = adamw(up_weight, up_moment, up_second, grad_gate_up[None, :, hidden_units:])
+    new_down = adamw(down_weight, down_moment, down_second, grad_down[None])
+    return (input_grad, prob_grad) + tuple(
+        value for trio in zip(new_gate, new_up, new_down) for value in trio
+    )
+
+
 def solution(mesh):
+    shape = dict(mesh.shape)
+    small = shape["dp"] == 8 and shape["expert"] == 4
     return jax.shard_map(
-        body,
+        block_body if small else body,
         mesh=mesh,
         in_specs=(
             P(("dp", "expert"), None),

time: 671 us -> 336 us (0.50); the launches traced: 663 us -> 335 us
  waiting for transfers between devices: 295 us -> 0 us
  Pallas kernels: 0 us -> 242 us
  local copies, waits for them, and re-layouts: 158 us -> 2.55 us
  blocking collectives: 49.9 us -> 0 us
  other arithmetic: 63.9 us -> 21.2 us
  starting transfers between devices: 20.9 us -> 0 us
  between operations: 14.2 us -> 0.79 us
    pallas_call x0 -> x2, Pallas kernels: none -> 242 us  [the longest x1 137 us: block_body(): pl.pallas_call(functools.partial(gather_kernel, depth), out_shape=(jax.Sh...]
    unnamed x4 -> x0, waiting for transfers between devices: 206 us -> none
    all_to_all x4 -> x0, waiting for transfers between devices: 83.6 us -> none  [the longest x1 41.9 us: body(): lax.all_to_all(input_rows.reshape(exp_dev, groups, capacity, width), 'exp...]
    slice x4 -> x0, local copies, waits for them, and re-layouts: 64.4 us -> none  [the longest x1 42.4 us: body(): joined[0, :split_at].reshape(model_cols, exp_dev, 2 * hidden_units)]
    all_to_all x1 -> x0, blocking collectives: 49.9 us -> none  [body(): lax.all_to_all(send_grad, 'expert', split_axis=1, concat_axis=1, tiled=True)]
    reshape x7 -> x0, local copies, waits for them, and re-layouts: 32.1 us -> none  [the longest x1 18.1 us: body(): jnp.einsum('erc,erf->cef', cols, pre_grad, preferred_element_type=jnp.flo...]
    transpose x2 -> x0, local copies, waits for them, and re-layouts: 31.3 us -> none  [the longest x1 20.7 us: body(): jnp.einsum('erc,erf->cef', cols, pre_grad, preferred_element_type=jnp.flo...]
    concatenate x2 -> x1, other arithmetic: 25.3 us -> 1.5 us  [block_body(): jnp.concatenate((gate_weight[0], up_weight[0]), axis=1).astype(bf16)]
  transfers between devices with their start and end apart: 7 -> 0, of which waited for: 4 -> 0; matrix products, arithmetic and copies ran while one was open for 10% -> 0% of each run, Pallas kernels for 0% -> 0%
where the time goes in v1:
time: 336 us; the launch traced here: 335 us
  Pallas kernels  242 us (72%)
  matrix products  68.5 us (20%)
  other arithmetic  21.2 us (6%)
    pallas_call x1, Pallas kernels, block_body(): pl.pallas_call(functools.partial(gather_kernel, depth), out_shape=(jax.Sh...  137 us
    pallas_call x1, Pallas kernels, block_body(): pl.pallas_call(functools.partial(scatter_kernel, depth), out_shape=(jax.S...  105 us
    dot_general x1, matrix products, block_body(): lax.dot_general(x_rows, pre_grad, tn, preferred_element_type=f32)  14.4 us
    dot_general x1, matrix products, block_body(): pre = jnp.dot(x_rows, w_gate_up, preferred_element_type=f32)  14.2 us
    dot_general x1, matrix products, block_body(): lax.dot_general(pre_grad, w_gate_up, nt, preferred_element_type=f32)  13.9 us
    dot_general x1, matrix products, block_body(): lax.dot_general(out_scaled, w_down, nt, preferred_element_type=f32)  13.3 us
    sub x2, other arithmetic, adamw(): weight - learn_rate * (update + decay_rate * weight)  12.3 us

profile of v1, /device:TPU:0, one launch (start us, length us, event | category | flops | bytes accessed | tf_op | source)
XLA Modules:
  0.0 335.3 jit_solution(2556960127504577942)
XLA Ops:
  0.6 2.4 convert_bitcast_fusion.1
  3.0 0.0 copy-start
  3.0 1.5 pad_maximum_fusion.3.wgu
  4.5 0.7 copy-done
  5.3 1.0 convert_bitcast_fusion.wd
  6.3 0.7 copy.31.gm
  7.1 137.4 %shard_map.212 = (bf16[2560,3072]{1,0:T(8,128)(2,1)}, bf16[1536,2560]{1,0:T(8,128)(2,1)}, bf16[512,2560]{1,0:T(8,128)(2,1)}, bf16[512,2560]{1,0:T(8,128)(2,1)}, bf16[512,128]{1,0:T(8,128)(2,1)}) custom-call(bf16[128,2560]{1,0:T(8,128)(2,1)} %x.1, bf16[128,2560]{1,0:T(8,128)(2,1)} %y.1, bf16[128,128]{1,0:T(8,128)(2,1)} %copy.31.gm, ...), custom_call_target="tpu_custom_call" | custom-call | tf_op jit(solution)/shard_map/pallas_call | solution.py:523
  144.5 14.2 %fusion.17 = f32[512,3072]{1,0:T(8,128)} fusion(bf16[512,2560]{1,0:T(8,128)(2,1)} %get-tuple-element.20, bf16[2560,3072]{1,0:T(8,128)(2,1)} %get-tuple-element.24), kind=kOutput, calls=%fused_computation.41 | convolution fusion | flops 8053063680 | bytes 24641536 | tf_op jit(solution)/shard_map/dot_general | solution.py:549
  158.7 0.1 select_reduce_fusion
  158.8 13.3 %multiply_convert_fusion.2 = (bf16[512,1536]{1,0:T(8,128)(2,1)}, bf16[512,1536]{1,0:T(8,128)(2,1)}, bf16[512,1536]{1,0:T(8,128)(2,1)}) fusion(f32[512,3072]{1,0:T(8,128)} %fusion.17, bf16[1536,2560]{1,0:T(8,128)(2,1)} %get-tuple-element.23, bf16[512,2560]{1,0:T(8,128)(2,1)} %get-tuple-element.22, f32[512]{0:T(512)S(1)} %select_reduce_fusion), kind=kOutput, calls=%fused_computation.10 | convolution fusion | flops 4042260480 | bytes 21497856 | tf_op jit(solution)/shard_map/dot_general | solution.py:558
  172.2 13.9 %convolution_convert_fusion.2.xr = bf16[512,2560]{1,0:T(8,128)(2,1)} fusion(bf16[2560,3072]{1,0:T(8,128)(2,1)} %get-tuple-element.24, bf16[512,1536]{1,0:T(8,128)(2,1)} %get-tuple-element.39, bf16[512,1536]{1,0:T(8,128)(2,1)} %get-tuple-element.38), kind=kOutput, calls=%fused_computation.6 | convolution fusion | flops 8060665856 | bytes 21495808 | tf_op jit(solution)/shard_map/dot_general | solution.py:563
  186.1 14.4 %convolution_convert_fusion.p13 = bf16[2560,3072]{1,0:T(8,128)(2,1)} fusion(bf16[512,2560]{1,0:T(8,128)(2,1)} %get-tuple-element.20, bf16[512,1536]{1,0:T(8,128)(2,1)} %get-tuple-element.39, bf16[512,1536]{1,0:T(8,128)(2,1)} %get-tuple-element.38), kind=kOutput, calls=%fused_computation | convolution fusion | flops 8067219456 | bytes 21495808 | tf_op jit(solution)/shard_map/dot_general | solution.py:564
  200.4 6.2 %fusion.1 = bf16[512]{0:T(512)(128)(2,1)S(1)} fusion(bf16[512,2560]{1,0:T(8,128)(2,1)S(1)} %copy-done.11, bf16[512,1536]{1,0:T(8,128)(2,1)} %get-tuple-element.40, bf16[1536,2560]{1,0:T(8,128)(2,1)S(1)} %bitcast.41), kind=kOutput, calls=%fused_computation.5 | convolution fusion | flops 4030463488 | bytes 12059648 | tf_op jit(solution)/shard_map/dot_general | solution.py:554
  206.6 0.8 broadcast_in_dim.55.q
  207.4 6.6 %convolution_convert_fusion.1.p2 = bf16[1536,2560]{1,0:T(8,128)(2,1)} fusion(bf16[512,1536]{1,0:T(8,128)(2,1)S(1)} %copy-done.12, bf16[512,2560]{1,0:T(8,128)(2,1)S(1)} %copy-done.11, f32[512]{0:T(512)S(1)} %select_reduce_fusion), kind=kOutput, calls=%fused_computation.1 | convolution fusion | flops 4034396160 | bytes 12060672 | tf_op jit(solution)/shard_map/dot_general | solution.py:565
  214.0 104.9 %shard_map.213 = (f32[320,3072]{1,0:T(8,128)}, f32[192,2560]{1,0:T(8,128)}, bf16[4,128,2560]{2,1,0:T(8,128)(2,1)}, bf16[4,128,128]{2,1,0:T(8,128)(2,1)}) custom-call(bf16[2560,3072]{1,0:T(8,128)(2,1)} %convolution_convert_fusion.p13, bf16[1536,2560]{1,0:T(8,128)(2,1)} %convolution_convert_fusion.1.p2, bf16[512,2560]{1,0:T(8,128)(2,1)} %convolution_convert_fusion.2.xr, ...), custom_call_target="tpu_custom_call" | custom-call | tf_op jit(solution)/shard_map/pallas_call | solution.py:569
  318.9 0.0 copy-start.3
  318.9 0.0 copy-start.4
  319.0 8.7 %multiply_subtract_fusion.1 = (f32[1,320,1536]{2,1,0:T(8,128)}, f32[1,320,1536]{2,1,0:T(8,128)}, f32[1,320,1536]{2,1,0:T(8,128)}, f32[1,320,1536]{2,1,0:T(8,128)...) fusion(f32[1,320,1536]{2,1,0:T(8,128)S(1)} %copy-done.1, f32[320,3072]{1,0:T(8,128)} %get-tuple-element.27, ...), kind=kLoop, calls=%fused_computation.27 | loop fusion | flops 14745600 | bytes 27525120 | tf_op jit(solution)/shard_map/sub | solution.py:34
  327.6 0.2 copy-done.5
  327.9 3.6 %multiply_subtract_fusion = (f32[1,192,2560]{2,1,0:T(8,128)}, f32[1,192,2560]{2,1,0:T(8,128)}, f32[1,192,2560]{2,1,0:T(8,128)}) fusion(f32[1,192,2560]{2,1,0:T(8,128)S(1)} %copy-done, f32[192,2560]{1,0:T(8,128)S(1)} %copy-done.5, f32[1,192,2560]{2,1,0:T(8,128)S(1)} %copy-done.3, f32[1,192,2560]{2,1,0:T(8,128)S(1)} %copy-done.4), kind=kLoop, calls=%fused_computation.26 | loop fusion | flops 7372800 | bytes 13762560 | tf_op jit(solution)/shard_map/sub | solution.py:34
  331.5 3.1 reduce_sum.54
  334.7 0.1 convert_reduce_fusion
  334.8 0.5 select_reduce_fusion.2
  (29 shorter events, 0.1 us)
Async XLA Ops:
  3.0 2.3 copy-start
  5.3 1.0 copy-start.9
  5.3 1.1 copy-start.10
  144.5 14.2 %copy-start.8 = (bf16[512,128]{1,0:T(8,128)(2,1)S(1)}, bf16[512,128]{1,0:T(8,128)(2,1)}, u32[]{:S(2)}) copy-start(bf16[512,128]{1,0:T(8,128)(2,1)} %get-tuple-element.21) | copy-start | bytes 393220
  158.8 41.6 %slice-start = ((s8[7864320]{0:T(1024)(128)(4,1)}), s8[4194304]{0:T(1024)(128)(4,1)S(1)}, s32[]{:S(2)}) async-start(s8[7864320]{0:T(1024)(128)(4,1)} %bitcast.40), calls=%async_computation | async-start | bytes 8388608
  172.2 28.3 %slice-start.1 = ((s8[7864320]{0:T(1024)(128)(4,1)}), s8[3670016]{0:T(1024)(128)(4,1)S(1)}, s32[]{:S(2)}) async-start(s8[7864320]{0:T(1024)(128)(4,1)} %bitcast.40), calls=%async_computation.1 | async-start | bytes 7340032
  186.1 14.4 %copy-start.11 = (bf16[512,2560]{1,0:T(8,128)(2,1)S(1)}, bf16[512,2560]{1,0:T(8,128)(2,1)}, u32[]{:S(2)}) copy-start(bf16[512,2560]{1,0:T(8,128)(2,1)} %get-tuple-element.22) | copy-start | bytes 7864324
  200.4 7.0 %copy-start.12 = (bf16[512,1536]{1,0:T(8,128)(2,1)S(1)}, bf16[512,1536]{1,0:T(8,128)(2,1)}, u32[]{:S(2)}) copy-start(bf16[512,1536]{1,0:T(8,128)(2,1)} %get-tuple-element.40) | copy-start | bytes 4718596
  214.0 104.9 %copy-start.1 = (f32[1,320,1536]{2,1,0:T(8,128)S(1)}, f32[1,320,1536]{2,1,0:T(8,128)}, u32[]{:S(2)}) copy-start(f32[1,320,1536]{2,1,0:T(8,128)} %param.18) | copy-start | bytes 5898244
  214.0 104.9 %copy-start.2 = (f32[1,320,1536]{2,1,0:T(8,128)S(1)}, f32[1,320,1536]{2,1,0:T(8,128)}, u32[]{:S(2)}) copy-start(f32[1,320,1536]{2,1,0:T(8,128)} %param.17) | copy-start | bytes 5898244
  214.0 104.9 %copy-start.6 = (f32[1,320,1536]{2,1,0:T(8,128)S(1)}, f32[1,320,1536]{2,1,0:T(8,128)}, u32[]{:S(2)}) copy-start(f32[1,320,1536]{2,1,0:T(8,128)} %param.21) | copy-start | bytes 5898244
  318.9 8.7 %copy-start.3 = (f32[1,192,2560]{2,1,0:T(8,128)S(1)}, f32[1,192,2560]{2,1,0:T(8,128)}, u32[]{:S(2)}) copy-start(f32[1,192,2560]{2,1,0:T(8,128)} %param.22) | copy-start | bytes 5898244
  318.9 8.7 %copy-start.4 = (f32[1,192,2560]{2,1,0:T(8,128)S(1)}, f32[1,192,2560]{2,1,0:T(8,128)}, u32[]{:S(2)}) copy-start(f32[1,192,2560]{2,1,0:T(8,128)} %param.25) | copy-start | bytes 5898244
  319.0 8.9 %copy-start.5 = (f32[192,2560]{1,0:T(8,128)S(1)}, f32[192,2560]{1,0:T(8,128)}, u32[]{:S(2)}) copy-start(f32[192,2560]{1,0:T(8,128)} %get-tuple-element.28) | copy-start | bytes 5898244
  331.5 3.1 copy-start.7
